TPU v7x, 1024 devices: a whole 4x4x32 slice. The times are simulated.
1024 devices in a mesh: rep: 64 (over z, core), tp: 16 (over y, x).
Axes of the slice: x: 4, y: 4, z: 32, core: 2. Of those that a mesh axis runs over, the one named last changes fastest.
Arguments:
- hidden: bfloat16 [16384, 8192], P('rep', 'tp'), may hold values from -6 to 6
- projection: bfloat16 [8192, 2048], P('tp'), may hold values from -0.0625 to 0.0625
- block_index: int32 [64, 2], P('rep'), may hold values from 0 to 1023
- block_counts: int32 [64], P('rep'), may hold values from 0 to 2, as said below
- block_change: bfloat16 [64, 2, 128, 128], P('rep'), may hold values from -0.0625 to 0.0625
- queries: bfloat16 [16384, 8192], P(('rep', 'tp')), may hold values from -160 to 160
- cached: bfloat16 [16384, 32, 2048], P(('rep', 'tp')), may hold values from -16 to 16
- lengths: int32 [16384], P(('rep', 'tp')), may hold values from 2 to 32, as said below
Outputs:
- new_entries: bfloat16 [16384, 2048], P(('rep', 'tp'))
- attention: bfloat16 [16384, 8192], P(('rep', 'tp'))
Inputs may be any that keep to these rules, and one draw needn't show every extreme that they name: `block_counts`: each learner shard uses at most 2 slots, and some shard uses 2. `lengths`: some row has 32 valid positions.
All inputs are finite; a program needn't handle non-finite values.
Results may differ from a plain program's by a relative error of at most 0.005.
Values may be sent and summed in bfloat16 or wider, within the bound.
A program may use at most 64 MiB of HBM per device.

v0:
```python
import math

import jax
import jax.numpy as jnp
from jax import lax
from jax.sharding import PartitionSpec as P

QH = 64
KVH = 8
HD = 128
BLK = 128
SLOTS = 2
GROUP = 8


def attend(query_rows, cached_rows, length_rows, new_rows):
    row_count = query_rows.shape[0]
    span = cached_rows.shape[1]
    score_scale = 1.0 / math.sqrt(HD)
    query_heads = query_rows.reshape(row_count, KVH, GROUP, HD)
    cache_keys = cached_rows[:, :, : KVH * HD].reshape(row_count, span, KVH, HD)
    cache_values = cached_rows[:, :, KVH * HD :].reshape(row_count, span, KVH, HD)
    own_keys = new_rows[:, : KVH * HD].reshape(row_count, KVH, HD)
    own_values = new_rows[:, KVH * HD :].reshape(row_count, KVH, HD)
    scores = (
        jnp.einsum("rkgd,rpkd->rkgp", query_heads, cache_keys, preferred_element_type=jnp.float32)
        * score_scale
    )
    own_scores = (
        jnp.einsum("rkgd,rkd->rkg", query_heads, own_keys, preferred_element_type=jnp.float32)
        * score_scale
    )
    visible = (jnp.arange(span, dtype=jnp.int32)[None, :] < length_rows[:, None])[:, None, None, :]
    masked = jnp.where(visible, scores, -jnp.inf)
    row_top = jnp.maximum(jnp.max(masked, axis=-1), own_scores)
    exp_terms = jnp.exp(masked - row_top[..., None])
    own_terms = jnp.exp(own_scores - row_top)
    denominator = jnp.sum(exp_terms, axis=-1) + own_terms
    weights = (exp_terms / denominator[..., None]).astype(jnp.bfloat16)
    own_weight = (own_terms / denominator).astype(jnp.bfloat16)
    mixed = jnp.einsum("rkgp,rpkd->rkgd", weights, cache_values, preferred_element_type=jnp.float32)
    mixed = (
        mixed
        + own_weight.astype(jnp.float32)[..., None] * own_values.astype(jnp.float32)[:, :, None, :]
    )
    return mixed.reshape(row_count, QH * HD).astype(jnp.bfloat16)


def body(hidden, projection, block_index, block_counts, block_change, queries, cached, lengths):
    group_rows = hidden.shape[0]
    weight_rows = projection.shape[0]
    weight_cols = projection.shape[1]
    row_blocks = weight_rows // BLK
    col_blocks = weight_cols // BLK
    column_blocks = row_blocks * col_blocks
    my_column = lax.axis_index("tp")
    hidden_blocks = hidden.reshape(group_rows, row_blocks, BLK)
    list_index, list_counts, list_change = (
        lax.all_gather(block_index, "rep", axis=0, tiled=True),
        lax.all_gather(block_counts, "rep", axis=0, tiled=True),
        lax.all_gather(block_change, "rep", axis=0, tiled=True),
    )
    live_slots = jnp.arange(SLOTS, dtype=jnp.int32)[None, :] < list_counts[:, None]
    local_index = list_index - my_column * column_blocks
    target = jnp.arange(column_blocks, dtype=jnp.int32)
    onehot = ((local_index[:, :, None] == target[None, None, :]) & live_slots[:, :, None]).astype(
        jnp.bfloat16
    )
    onehot = onehot.reshape(-1, column_blocks)
    flattened = list_change.reshape(-1, BLK * BLK)
    column_change = jnp.einsum("sb,sq->bq", onehot, flattened, preferred_element_type=jnp.float32)
    column_change = column_change.reshape(row_blocks, col_blocks, BLK, BLK)
    upper_part = column_change.astype(jnp.bfloat16)
    lower_part = (column_change - upper_part.astype(jnp.float32)).astype(jnp.bfloat16)
    correction = jnp.einsum(
        "rad,acde->rce", hidden_blocks, upper_part, preferred_element_type=jnp.float32
    )
    correction = correction + jnp.einsum(
        "rad,acde->rce", hidden_blocks, lower_part, preferred_element_type=jnp.float32
    )
    correction = correction.reshape(group_rows, weight_cols)
    kv_sum = lax.psum_scatter(
        jnp.dot(hidden, projection, preferred_element_type=jnp.float32) + correction,
        "tp",
        scatter_dimension=0,
        tiled=True,
    )
    new_entries = kv_sum.astype(jnp.bfloat16)
    attention = attend(queries, cached, lengths, new_entries)
    return (new_entries, attention)


def solution(mesh):
    return jax.shard_map(
        body,
        mesh=mesh,
        in_specs=(
            P("rep", "tp"),
            P("tp", None),
            P("rep", None),
            P("rep"),
            P("rep", None, None, None),
            P(("rep", "tp"), None),
            P(("rep", "tp"), None, None),
            P(("rep", "tp")),
        ),
        out_specs=(P(("rep", "tp"), None), P(("rep", "tp"), None)),
        check_vma=False,
    )
```

profile of v0, /device:TPU:1, one launch (start us, length us, event | category | flops | bytes accessed | tf_op | source)
XLA Modules:
  0.0 297.7 jit_solution(7111755129387888092)
XLA Ops:
  7.2 0.0 copy-start
  7.2 0.0 all-gather.3.cloned.1.call-start
  7.2 0.7 all-gather.3.cloned.1.call-update
  7.9 0.0 reduce-scatter.2.cloned.1.call-start
  8.0 69.9 %all-gather = s32[64,1,2]{2,1,0:T(1,128)S(1)} all-gather(s32[1,1,2]{2,1,0:T(1,128)} %bitcast.87), channel_id=1, replica_groups=mesh['rep'=64,'tp'=16] {'rep'}, dimensions={0}, use_global_device_ids=true | all-gather | bytes 520 | tf_op jit(solution)/shard_map/all_gather | solution.py:59
  77.9 0.1 subtract_reduce_fusion
  78.0 0.1 eq.32
  78.8 1.3 dynamic-slice
  80.1 0.8 dynamic-update-slice
  80.8 25.8 %all-reduce = s32[64]{0:T(128)S(1)} all-reduce(s32[64]{0:T(128)S(1)} %dynamic-update-slice), channel_id=1, replica_groups=mesh['rep'=64,'tp'=16] {'rep'}, use_global_device_ids=true, to_apply=%add | all-reduce | flops 64 | bytes 512
  106.6 0.1 iota_compare_fusion
  106.6 0.2 lt.40
  106.8 52.0 %all-gather.3.cloned.1.call-done = bf16[64,2,128,128]{3,2,1,0:T(8,128)(2,1)} async-done(((bf16[1,2,128,128]{3,2,1,0:T(8,128)(2,1)}), bf16[64,2,128,128]{3,2,1,0:T(8,128)(2,1)}) %all-gather.3.cloned.1.call-update) | async-done | bytes 4194320 | tf_op jit(solution)/shard_map/all_gather | solution.py:61
  158.8 7.7 %copy.71 = bf16[16,8,128,128]{3,1,2,0:T(8,128)(2,1)} copy(bf16[16,8,128,128]{3,2,1,0:T(8,128)(2,1)} %bitcast.78) | data formatting | bytes 8388608
  166.5 6.4 %copy.24 = bf16[128,16384]{0,1:T(8,128)(2,1)} copy(bf16[128,16384]{1,0:T(8,128)(2,1)} %bitcast.76) | data formatting | bytes 8388608 | tf_op jit(solution)/shard_map/reshape | solution.py:70
  172.9 3.9 %subtract_convert_fusion = (bf16[4,16,128,128]{3,1,2,0:T(8,128)(2,1)S(1)}, bf16[4,16,128,128]{3,1,2,0:T(8,128)(2,1)S(1)}) fusion(bf16[128,128,128,1]{2,1,0,3:T(8,128)(2,1)} %bitcast.75, s32[4,16]{1,0:T(4,128)S(1)} %multiply_add_fusion, s32[128]{0:T(128)S(1)} %eq.32, pred[128]{0:T(512)(128)(4,1)S(1)} %lt.40), kind=kOutput, calls=%fused_computation.1 | convolution fusion | flops 272646144 | bytes 8389504 | tf_op jit(solution)/shard_map/sb,sq->bq/dot_general | solution.py:71
  176.8 1.2 fusion
  177.9 2.6 bitcast_add_fusion
  180.5 2.9 copy.37
  183.4 0.0 copy-done
  183.4 3.6 %convolution_add_fusion = f32[256,2048]{1,0:T(8,128)} fusion(f32[256,2048]{1,0:T(8,128)} %copy.37, bf16[256,512]{1,0:T(8,128)(2,1)S(1)} %copy-done.1, bf16[512,2048]{1,0:T(8,128)(2,1)S(1)} %copy-done), kind=kOutput, calls=%fused_computation.2 | convolution fusion | flops 537395200 | bytes 6553600 | tf_op jit(solution)/shard_map/dot_general | solution.py:83
  187.0 0.0 reduce-scatter.2.cloned.1.call-update
  187.0 0.9 copy-done.3
  188.0 0.1 iota_compare_fusion.1
  188.1 2.7 slice_bitcast_fusion.1
  190.8 0.7 fusion.27
  191.5 95.0 %reduce-scatter.2.cloned.1.call-done = f32[16,2048]{1,0:T(8,128)} async-done(((f32[256,2048]{1,0:T(8,128)}), f32[16,2048]{1,0:T(8,128)}) %reduce-scatter.2.cloned.1.call-update) | async-done | bytes 131088 | tf_op jit(solution)/shard_map/reduce_scatter | solution.py:82
  286.5 0.9 convert_element_type.41
  287.5 0.3 fusion.28
  287.8 0.4 fusion.12
  288.3 1.7 fusion.7
  290.0 0.9 copy.72
  (15 shorter events, 0.2 us)
Async XLA Ops:
  7.2 176.2 %copy-start = (bf16[512,2048]{1,0:T(8,128)(2,1)S(1)}, bf16[512,2048]{1,0:T(8,128)(2,1)}, u32[]{:S(2)}) copy-start(bf16[512,2048]{1,0:T(8,128)(2,1)} %param.9) | copy-start | bytes 6291460
  7.2 151.7 %all-gather.3.cloned.1.call-start = ((), (), s32[]{:S(2)}) async-start(), calls=%async_computation.1 | async-start | bytes 4259840 | tf_op jit(solution)/shard_map/all_gather | solution.py:61
  7.9 278.6 %reduce-scatter.2.cloned.1.call-start = ((), (), s32[]{:S(2)}) async-start(), calls=%async_computation.2 | async-start | bytes 2228224 | tf_op jit(solution)/shard_map/reduce_scatter | solution.py:82
  172.9 3.9 %copy-start.1 = (bf16[256,512]{1,0:T(8,128)(2,1)S(1)}, bf16[256,512]{1,0:T(8,128)(2,1)}, u32[]{:S(2)}) copy-start(bf16[256,512]{1,0:T(8,128)(2,1)} %param.8) | copy-start | bytes 786436
  187.0 0.9 copy-start.3
  187.0 1.0 copy-start.4
  287.5 2.6 copy-start.2
Sparse Core Ops, SparseCore 0:
  10.7 148.0 all-gather.2
  187.2 99.3 reduce-scatter.1
where the time goes:
time: 299 us; the launch traced here: 298 us
  waiting for transfers between devices  148 us (49%)
  blocking collectives  95.7 us (32%)
  local copies, waits for them, and re-layouts  23.9 us (8%)
  between operations  14.8 us (5%)
  matrix products  13.9 us (5%)
    reduce_scatter x1, waiting for transfers between devices, body(): lax.psum_scatter(jnp.dot(hidden, projection, preferred_element_type=jnp.f...  95 us
    all_gather x1, blocking collectives, body(): lax.all_gather(block_index, 'rep', axis=0, tiled=True)  69.9 us
    all_gather x1, waiting for transfers between devices, body(): lax.all_gather(block_change, 'rep', axis=0, tiled=True)  52 us
    unnamed x1, blocking collectives  25.8 us
    unnamed x18, local copies, waits for them, and re-layouts  14.3 us
    reshape x1, local copies, waits for them, and re-layouts, body(): flattened = list_change.reshape(-1, BLK * BLK)  6.39 us
  transfers between devices with their start and end apart: 2, of which 2 were waited for; matrix products, arithmetic and copies ran while one was open for 2% of the time, Pallas kernels for 0%

commit v1 on v0

v1 whole, which is shorter than its diff:
```python
import functools
import math

import jax
import jax.numpy as jnp
from jax import lax
from jax.experimental import pallas as pl
from jax.experimental.pallas import tpu as pltpu
from jax.sharding import PartitionSpec as P

QH = 64
KVH = 8
HD = 128
BLK = 128
SLOTS = 2
GROUP = 8
MESH = pl.DeviceIdType.MESH
BF = jnp.bfloat16
F32 = jnp.float32
NEG = -1e30
NT = (((1,), (1,)), ((), ()))
TN = (((0,), (0,)), ((), ()))


def iota(shape, dim):
    return lax.broadcasted_iota(jnp.int32, shape, dim)


def kernel(
    n_rep,
    n_tp,
    nx,
    zlo_n,
    chunks,
    hid_hbm,
    proj_hbm,
    idx_ref,
    cnt_ref,
    chg_hbm,
    q_hbm,
    cache_hbm,
    len_ref,
    new_ref,
    att_ref,
    hid,
    proj,
    chg,
    qs,
    cache,
    gath,
    meta,
    perm,
    hp,
    hs,
    hsm,
    d32,
    dd,
    dense,
    acc,
    sendbuf,
    recv,
    bias,
    mixed,
    mstat,
    lstat,
    local_sem,
    s1_send,
    s1_recv,
    s2_send,
    s2_recv,
    s3_send,
    s3_recv,
    hs_send,
    hs_recv,
    rs_send,
    rs_recv,
):
    rep = lax.axis_index("rep")
    tp = lax.axis_index("tp")
    core = rep % 2
    z = rep // 2
    nz = n_rep // 2
    zhi_n = nz // zlo_n
    zlo = z % zlo_n
    zhi = z // zlo_n
    ny = n_tp // nx
    y = tp // nx
    x = tp % nx
    ks = BLK // n_tp
    depth = hid.shape[1]
    rows = hid.shape[0]
    nrb = depth // BLK
    kvw = proj.shape[1]
    own_rows = rows // n_tp
    slots = n_rep * SLOTS
    share = nrb * ks
    cw = kvw // chunks
    ncb = kvw // BLK

    loads = []
    for n, (src, dst) in enumerate(
        ((chg_hbm, chg), (hid_hbm, hid), (proj_hbm, proj), (q_hbm, qs), (cache_hbm, cache))
    ):
        copy = pltpu.make_async_copy(src, dst, local_sem.at[n])
        copy.start()
        loads.append(copy)

    sign = 1 - 2 * core

    def at_z(zz, cc):
        return {"rep": ((zz + 2 * nz) % nz) * 2 + cc, "tp": tp}

    def plane(o, direction):
        oy, ox = o // nx, o % nx
        return ((y + direction * oy + ny) % ny) * nx + (x + direction * ox + nx) % nx

    strides = list(range(1, zhi_n))
    steps = [d for d in range(-(zlo_n // 2 - 1), zlo_n // 2 + 1) if d != 0]

    barrier = pltpu.get_barrier_semaphore()
    for j in strides:
        pl.semaphore_signal(barrier, inc=1, device_id=at_z(z - zlo_n * j, core), device_id_type=MESH)
    for d in steps:
        pl.semaphore_signal(barrier, inc=1, device_id=at_z(z - sign * d, core), device_id_type=MESH)
    pl.semaphore_signal(barrier, inc=1, device_id=at_z(z, 1 - core), device_id_type=MESH)
    for o in range(1, n_tp):
        pl.semaphore_signal(
            barrier, inc=1, device_id={"rep": rep, "tp": plane(o, -1)}, device_id_type=MESH
        )

    place = (core * zlo_n + zlo) * zhi_n + zhi
    lane = iota((1, 128), 1)
    row_value = jnp.zeros((1, 128), F32)
    for s in range(SLOTS):
        b = idx_ref[0, s]
        target = (b & (ncb - 1)) * (n_tp * nrb) + (b >> 4) + 1
        target = jnp.where(s < cnt_ref[0], target, 0)
        row_value = jnp.where(lane == place * SLOTS + s, target.astype(F32), row_value)
    meta[core, zlo, zhi] = row_value

    pj = iota((SLOTS * ks, SLOTS * BLK), 0)
    pk = iota((SLOTS * ks, SLOTS * BLK), 1)
    pick = jnp.where(pk == (pj // ks) * BLK + tp * ks + pj % ks, 1.0, 0.0).astype(BF)
    loads[0].wait()
    own_share = jnp.dot(pick, chg[...].reshape(SLOTS * BLK, BLK), preferred_element_type=F32)
    gath[core, zlo, zhi] = own_share.astype(BF)

    pj = iota((depth, depth), 0)
    pk = iota((depth, depth), 1)
    perm[...] = jnp.where(
        pk == ((pj % share) // ks) * BLK + (pj // share) * ks + pj % ks, 1.0, 0.0
    ).astype(BF)

    pl.semaphore_wait(barrier, len(strides) + len(steps) + 1 + n_tp - 1)

    def s1_copies(j, send):
        zz = zhi if send else (zhi - j + zhi_n) % zhi_n
        dev = at_z(z + zlo_n * j, core)
        return [
            pltpu.make_async_remote_copy(
                src_ref=ref.at[core, zlo, zz],
                dst_ref=ref.at[core, zlo, zz],
                send_sem=s1_send.at[m, j - 1],
                recv_sem=s1_recv.at[m, j - 1],
                device_id=dev,
                device_id_type=MESH,
            )
            for m, ref in enumerate((gath, meta))
        ]

    def s2_copies(i, d, send):
        zz = zlo if send else (zlo - sign * d + zlo_n) % zlo_n
        dev = at_z(z + sign * d, core)
        return [
            pltpu.make_async_remote_copy(
                src_ref=ref.at[core, zz],
                dst_ref=ref.at[core, zz],
                send_sem=s2_send.at[m, i],
                recv_sem=s2_recv.at[m, i],
                device_id=dev,
                device_id_type=MESH,
            )
            for m, ref in enumerate((gath, meta))
        ]

    def s3_copies(send):
        cc = core if send else 1 - core
        return [
            pltpu.make_async_remote_copy(
                src_ref=ref.at[cc],
                dst_ref=ref.at[cc],
                send_sem=s3_send.at[m],
                recv_sem=s3_recv.at[m],
                device_id=at_z(z, 1 - core),
                device_id_type=MESH,
            )
            for m, ref in enumerate((gath, meta))
        ]

    for j in strides:
        for copy in s1_copies(j, True):
            copy.start()

    loads[1].wait()
    hp[...] = lax.dot_general(perm[...], hid[...], NT, preferred_element_type=F32).astype(BF).reshape(hp.shape)
    hs[0] = hp[tp]
    for o in range(1, n_tp):
        dest = plane(o, 1)
        pltpu.make_async_remote_copy(
            src_ref=hp.at[dest],
            dst_ref=hs.at[o],
            send_sem=hs_send,
            recv_sem=hs_recv,
            device_id={"rep": rep, "tp": dest},
            device_id_type=MESH,
        ).start()

    for j in strides:
        for copy in s1_copies(j, False):
            copy.wait_recv()
    for i, d in enumerate(steps):
        for copy in s2_copies(i, d, True):
            copy.start()

    loads[2].wait()
    tile = 512

    @pl.loop(0, kvw // tile)
    def _(n):
        cols = pl.ds(pl.multiple_of(n * tile, tile), tile)
        acc[:, cols] = jnp.dot(hid[...], proj[:, cols], preferred_element_type=F32)

    pj = iota((depth, depth), 0)
    pk = iota((depth, depth), 1)
    po = pj // share
    pc = ((y - po // nx + ny) % ny) * nx + (x - po % nx + nx) % nx
    perm[...] = jnp.where(
        pk == (pj % ks) * (n_tp * nrb) + pc * nrb + (pj % share) // ks, 1.0, 0.0
    ).astype(BF)

    def hs_wait():
        return pltpu.make_async_remote_copy(
            src_ref=hs.at[pl.ds(1, n_tp - 1)],
            dst_ref=hs.at[pl.ds(1, n_tp - 1)],
            send_sem=hs_send,
            recv_sem=hs_recv,
            device_id={"rep": rep, "tp": plane(1, 1)},
            device_id_type=MESH,
        )

    for i, d in enumerate(steps):
        for copy in s2_copies(i, d, False):
            copy.wait_recv()
    for copy in s3_copies(True):
        copy.start()

    hs_wait().wait_recv()
    hsm[...] = lax.dot_general(
        hs[...].reshape(depth, rows), perm[...], TN, preferred_element_type=F32
    ).astype(BF)

    for copy in s3_copies(False):
        copy.wait_recv()

    target_row = jnp.sum(meta[...].reshape(n_rep, 128), axis=0, keepdims=True)[:, :slots]
    d32[...] = gath[...].reshape(slots * ks, BLK).astype(F32)
    for k in range(ks):
        dd[:, k * BLK : (k + 1) * BLK] = d32[pl.ds(k, slots, stride=ks), :].astype(BF)

    per = cw // BLK
    grp = n_tp * nrb

    @pl.loop(0, chunks)
    def _(n):
        first = n * (per * grp) + 1
        ids = (iota((per * grp, slots), 0) + first).astype(F32)
        onehot = jnp.where(ids == target_row, 1.0, 0.0).astype(BF)
        for k in range(ks):
            placed = jnp.dot(
                onehot, dd[:, k * BLK : (k + 1) * BLK], preferred_element_type=F32
            ).astype(BF)
            for c in range(per):
                dense[k * grp : (k + 1) * grp, c * BLK : (c + 1) * BLK] = placed[
                    c * grp : (c + 1) * grp
                ]
        cols = pl.ds(pl.multiple_of(n * cw, cw), cw)
        total = acc[:, cols] + jnp.dot(hsm[...], dense[...], preferred_element_type=F32)
        acc[:, cols] = total
        sendbuf[n] = total.astype(BF).reshape(n_tp, own_rows, cw)
        for o in range(1, n_tp):
            dest = plane(o, 1)
            pltpu.make_async_remote_copy(
                src_ref=sendbuf.at[n, dest],
                dst_ref=recv.at[n, o - 1],
                send_sem=rs_send.at[n],
                recv_sem=rs_recv.at[n],
                device_id={"rep": rep, "tp": dest},
                device_id_type=MESH,
            ).start()

    def rs_wait(n):
        return pltpu.make_async_remote_copy(
            src_ref=recv.at[n],
            dst_ref=recv.at[n],
            send_sem=rs_send.at[n],
            recv_sem=rs_recv.at[n],
            device_id={"rep": rep, "tp": plane(1, 1)},
            device_id_type=MESH,
        )

    scale = 1.0 / math.sqrt(HD)
    loads[3].wait()
    loads[4].wait()
    span = cache.shape[1]
    positions = own_rows * span
    pos_lane = iota((1, positions), 1)
    valid_len = jnp.zeros((1, positions), jnp.int32)
    for i in range(own_rows):
        valid_len = jnp.where(pos_lane // span == i, len_ref[i], valid_len)
    seen = jnp.where(pos_lane % span < valid_len, 0.0, NEG)
    same = iota((GROUP * own_rows, positions), 0) % own_rows == iota(
        (GROUP * own_rows, positions), 1
    ) // span
    bias[...] = jnp.where(same, seen, NEG)

    def head_queries(k):
        heads = qs[:, pl.ds(pl.multiple_of(k * GROUP * HD, GROUP * HD), GROUP * HD)]
        return jnp.concatenate([heads[:, g * HD : (g + 1) * HD] for g in range(GROUP)], axis=0)

    @pl.loop(0, KVH)
    def _(k):
        keys = cache[:, :, pl.ds(pl.multiple_of(k * HD, HD), HD)].reshape(positions, HD)
        values = cache[:, :, pl.ds(pl.multiple_of((KVH + k) * HD, HD), HD)].reshape(positions, HD)
        score = lax.dot_general(head_queries(k), keys, NT, preferred_element_type=F32)
        score = score * scale + bias[...]
        top = jnp.max(score, axis=1, keepdims=True)
        e = jnp.exp(score - top)
        hi = e.astype(BF)
        lo = (e - hi.astype(F32)).astype(BF)
        mixed[k] = jnp.dot(hi, values, preferred_element_type=F32) + jnp.dot(
            lo, values, preferred_element_type=F32
        )
        mstat[k] = jnp.broadcast_to(top, (GROUP * own_rows, HD))
        lstat[k] = jnp.broadcast_to(jnp.sum(e, axis=1, keepdims=True), (GROUP * own_rows, HD))

    mine = pl.ds(pl.multiple_of(tp * own_rows, own_rows), own_rows)
    for n in range(chunks):
        rs_wait(n).wait_recv()
        cols = slice(n * cw, (n + 1) * cw)
        total = acc[mine, cols]
        for o in range(n_tp - 1):
            total = total + recv[n, o].astype(F32)
        new_ref[:, cols] = total.astype(BF)

    @pl.loop(0, KVH)
    def _(k):
        own_key = new_ref[:, pl.ds(pl.multiple_of(k * HD, HD), HD)].astype(F32)
        own_value = new_ref[:, pl.ds(pl.multiple_of((KVH + k) * HD, HD), HD)].astype(F32)
        q = head_queries(k).astype(F32)
        own = jnp.sum(
            q * jnp.concatenate([own_key] * GROUP, axis=0), axis=1, keepdims=True
        ) * scale
        top = mstat[k]
        new_top = jnp.maximum(top, own)
        a = jnp.exp(top - new_top)
        b = jnp.exp(own - new_top)
        inv = 1.0 / (lstat[k] * a + b)
        out = mixed[k] * (a * inv) + (b * inv) * jnp.concatenate([own_value] * GROUP, axis=0)
        out = out.astype(BF)
        for g in range(GROUP):
            at = pl.multiple_of(k * GROUP * HD, GROUP * HD) + g * HD
            att_ref[:, pl.ds(pl.multiple_of(at, HD), HD)] = out[g * own_rows : (g + 1) * own_rows]

    for j in strides:
        for copy in s1_copies(j, True):
            copy.wait_send()
    for i, d in enumerate(steps):
        for copy in s2_copies(i, d, True):
            copy.wait_send()
    for copy in s3_copies(True):
        copy.wait_send()
    hs_wait().wait_send()
    for n in range(chunks):
        rs_wait(n).wait_send()


def solution(mesh):
    n_rep, n_tp = mesh.shape["rep"], mesh.shape["tp"]
    nx = 4 if n_tp == 16 else 2
    nz = n_rep // 2
    zlo_n = 8 if nz == 32 else 2
    zhi_n = nz // zlo_n
    chunks = 2

    def body(hidden, projection, block_index, block_counts, block_change, queries, cached, lengths):
        rows, depth = hidden.shape
        kvw = projection.shape[1]
        own_rows, span = cached.shape[0], cached.shape[1]
        ks = BLK // n_tp
        slots = n_rep * SLOTS
        share = depth // n_tp
        cw = kvw // chunks
        heads = GROUP * own_rows
        n1, n2 = zhi_n - 1, zlo_n - 1
        any_spec = pl.BlockSpec(memory_space=pl.ANY)
        smem = pl.BlockSpec(memory_space=pltpu.SMEM)
        vmem = pl.BlockSpec(memory_space=pltpu.VMEM)
        dma = pltpu.SemaphoreType.DMA
        return pl.pallas_call(
            functools.partial(kernel, n_rep, n_tp, nx, zlo_n, chunks),
            out_shape=(
                jax.ShapeDtypeStruct((own_rows, kvw), BF),
                jax.ShapeDtypeStruct((own_rows, queries.shape[1]), BF),
            ),
            in_specs=[any_spec, any_spec, smem, smem, any_spec, any_spec, any_spec, smem],
            out_specs=(vmem, vmem),
            scratch_shapes=[
                pltpu.VMEM((rows, depth), BF),
                pltpu.VMEM((depth, kvw), BF),
                pltpu.VMEM(block_change.shape, BF),
                pltpu.VMEM(queries.shape, BF),
                pltpu.VMEM(cached.shape, BF),
                pltpu.VMEM((2, zlo_n, zhi_n, SLOTS * ks, BLK), BF),
                pltpu.VMEM((2, zlo_n, zhi_n, 1, 128), F32),
                pltpu.VMEM((depth, depth), BF),
                pltpu.VMEM((n_tp, share, rows), BF),
                pltpu.VMEM((n_tp, share, rows), BF),
                pltpu.VMEM((rows, depth), BF),
                pltpu.VMEM((slots * ks, BLK), F32),
                pltpu.VMEM((slots, ks * BLK), BF),
                pltpu.VMEM((depth, cw), BF),
                pltpu.VMEM((rows, kvw), F32),
                pltpu.VMEM((chunks, n_tp, own_rows, cw), BF),
                pltpu.VMEM((chunks, n_tp - 1, own_rows, cw), BF),
                pltpu.VMEM((heads, own_rows * span), F32),
                pltpu.VMEM((KVH, heads, HD), F32),
                pltpu.VMEM((KVH, heads, HD), F32),
                pltpu.VMEM((KVH, heads, HD), F32),
                dma((5,)),
                dma((2, n1)),
                dma((2, n1)),
                dma((2, n2)),
                dma((2, n2)),
                dma((2,)),
                dma((2,)),
                dma,
                dma,
                dma((chunks,)),
                dma((chunks,)),
            ],
            compiler_params=pltpu.CompilerParams(
                collective_id=0, has_side_effects=True, vmem_limit_bytes=48 * 1024 * 1024
            ),
        )(hidden, projection, block_index, block_counts, block_change, queries, cached, lengths)

    return jax.shard_map(
        body,
        mesh=mesh,
        in_specs=(
            P("rep", "tp"),
            P("tp", None),
            P("rep", None),
            P("rep"),
            P("rep", None, None, None),
            P(("rep", "tp"), None),
            P(("rep", "tp"), None, None),
            P(("rep", "tp")),
        ),
        out_specs=(P(("rep", "tp"), None), P(("rep", "tp"), None)),
        check_vma=False,
    )
```

time: 299 us -> 75.9 us (0.25)
  waiting for transfers between devices: 148 us -> 0 us
  blocking collectives: 95.7 us -> 0 us
  Pallas kernels: 0 us -> 65.7 us
  local copies, waits for them, and re-layouts: 23.9 us -> 8.56 us
  matrix products: 13.9 us -> 0 us
  between operations: 14.8 us -> 1.3 us
    reduce_scatter x1 -> x0, waiting for transfers between devices: 95 us -> none  [body(): lax.psum_scatter(jnp.dot(hidden, projection, preferred_element_type=jnp.f...]
    all_gather x1 -> x0, blocking collectives: 69.9 us -> none  [body(): lax.all_gather(block_index, 'rep', axis=0, tiled=True)]
    pallas_call x0 -> x1, Pallas kernels: none -> 65.7 us  [body(): pl.pallas_call(functools.partial(kernel, n_rep, n_tp, nx, zlo_n, chunks),...]
    all_gather x1 -> x0, waiting for transfers between devices: 52 us -> none  [body(): lax.all_gather(block_change, 'rep', axis=0, tiled=True)]
    unnamed x1 -> x0, blocking collectives: 25.8 us -> none
    dot_general x7 -> x0, matrix products: 13.9 us -> none  [the longest x1 3.85 us: body(): jnp.einsum('sb,sq->bq', onehot, flattened, preferred_element_type=jnp.flo...]
    reshape x3 -> x0, local copies, waits for them, and re-layouts: 9.31 us -> none  [the longest x1 6.39 us: body(): flattened = list_change.reshape(-1, BLK * BLK)]
    unnamed x18 -> x16, local copies, waits for them, and re-layouts: 14.3 us -> 8.56 us
  transfers between devices with their start and end apart: 2 -> 0, of which waited for: 2 -> 0; matrix products, arithmetic and copies ran while one was open for 2% -> 0% of each run, Pallas kernels for 0% -> 0%
where the time goes in v1:
time: 75.9 us; the launch traced here: 75.6 us
  Pallas kernels  65.7 us (87%)
  local copies, waits for them, and re-layouts  8.56 us (11%)
  between operations  1.3 us (2%)
    pallas_call x1, Pallas kernels, body(): pl.pallas_call(functools.partial(kernel, n_rep, n_tp, nx, zlo_n, chunks),...  65.7 us
    unnamed x16, local copies, waits for them, and re-layouts  8.56 us

profile of v1, /device:TPU:1, one launch (start us, length us, event | category | flops | bytes accessed | tf_op | source)
XLA Modules:
  0.0 75.6 jit_solution(10003492466620381679)
XLA Ops:
  1.3 0.0 copy-start
  1.3 1.6 %copy-done = bf16[512,2048]{1,0:T(8,128)(2,1)S(1)} copy-done((bf16[512,2048]{1,0:T(8,128)(2,1)S(1)}, bf16[512,2048]{1,0:T(8,128)(2,1)}, u32[]{:S(2)}) %copy-start) | copy-done | bytes 2097176
  2.9 0.0 copy-start.1
  2.9 1.6 %copy-done.1 = bf16[16,32,2048]{2,1,0:T(8,128)(2,1)S(1)} copy-done((bf16[16,32,2048]{2,1,0:T(8,128)(2,1)S(1)}, bf16[16,32,2048]{2,1,0:T(8,128)(2,1)}, u32[]{:S(2)}) %copy-start.1) | copy-done | bytes 2097176
  4.5 0.0 copy-start.2
  4.5 0.9 %copy-done.2 = bf16[256,512]{1,0:T(8,128)(2,1)S(1)} copy-done((bf16[256,512]{1,0:T(8,128)(2,1)S(1)}, bf16[256,512]{1,0:T(8,128)(2,1)}, u32[]{:S(2)}) %copy-start.2) | copy-done | bytes 262168
  5.4 0.0 copy-start.3
  5.4 0.9 %copy-done.3 = bf16[16,8192]{1,0:T(8,128)(2,1)S(1)} copy-done((bf16[16,8192]{1,0:T(8,128)(2,1)S(1)}, bf16[16,8192]{1,0:T(8,128)(2,1)}, u32[]{:S(2)}) %copy-start.3) | copy-done | bytes 262168
  6.4 0.0 copy-start.4
  6.4 0.8 %copy-done.4 = bf16[1,2,128,128]{3,2,1,0:T(8,128)(2,1)S(1)} copy-done((bf16[1,2,128,128]{3,2,1,0:T(8,128)(2,1)S(1)}, bf16[1,2,128,128]{3,2,1,0:T(8,128)(2,1)}, u32[]{:S(2)}) %copy-start.4) | copy-done | bytes 65560
  7.2 0.0 copy-start.5
  7.2 0.7 copy-done.5
  7.9 0.0 copy-start.6
  7.9 0.7 copy-done.6
  8.5 65.7 %shard_map.95 = (bf16[16,2048]{1,0:T(8,128)(2,1)S(1)}, bf16[16,8192]{1,0:T(8,128)(2,1)S(1)}) custom-call(bf16[256,512]{1,0:T(8,128)(2,1)S(1)} %copy-done.2, bf16[512,2048]{1,0:T(8,128)(2,1)S(1)} %copy-done, s32[1,2]{1,0:T(1,128)S(1)} %copy-done.5, s32[1]{0:T(128)S(6)} %copy.12.cnt_ref, bf16[1,2,128,128]{3,2,1,0:T(8,128)(2,1)S(1)} %copy-done.4, ...), custom_call_target="tpu_custom_call" | custom-call | tf_op jit(solution)/shard_map/pallas_call | solution.py:409
  74.2 0.6 copy.13
  74.9 0.7 copy.14
Async XLA Ops:
  1.3 1.6 %copy-start = (bf16[512,2048]{1,0:T(8,128)(2,1)S(1)}, bf16[512,2048]{1,0:T(8,128)(2,1)}, u32[]{:S(2)}) copy-start(bf16[512,2048]{1,0:T(8,128)(2,1)} %proj_hbm.1) | copy-start | bytes 6291460
  2.9 1.6 %copy-start.1 = (bf16[16,32,2048]{2,1,0:T(8,128)(2,1)S(1)}, bf16[16,32,2048]{2,1,0:T(8,128)(2,1)}, u32[]{:S(2)}) copy-start(bf16[16,32,2048]{2,1,0:T(8,128)(2,1)} %cache_hbm.1) | copy-start | bytes 6291460
  4.5 0.9 %copy-start.2 = (bf16[256,512]{1,0:T(8,128)(2,1)S(1)}, bf16[256,512]{1,0:T(8,128)(2,1)}, u32[]{:S(2)}) copy-start(bf16[256,512]{1,0:T(8,128)(2,1)} %hid_hbm.1) | copy-start | bytes 786436
  5.4 0.9 %copy-start.3 = (bf16[16,8192]{1,0:T(8,128)(2,1)S(1)}, bf16[16,8192]{1,0:T(8,128)(2,1)}, u32[]{:S(2)}) copy-start(bf16[16,8192]{1,0:T(8,128)(2,1)} %q_hbm.1) | copy-start | bytes 786436
  6.4 0.8 %copy-start.4 = (bf16[1,2,128,128]{3,2,1,0:T(8,128)(2,1)S(1)}, bf16[1,2,128,128]{3,2,1,0:T(8,128)(2,1)}, u32[]{:S(2)}) copy-start(bf16[1,2,128,128]{3,2,1,0:T(8,128)(2,1)} %chg_hbm.1) | copy-start | bytes 196612
  7.2 0.7 copy-start.5
  7.9 0.7 copy-start.6

commit v2 on v1

v2 whole, which is shorter than its diff:
```python
import functools
import math

import jax
import jax.numpy as jnp
from jax import lax
from jax.experimental import pallas as pl
from jax.experimental.pallas import tpu as pltpu
from jax.sharding import PartitionSpec as P

QH = 64
KVH = 8
HD = 128
BLK = 128
SLOTS = 2
GROUP = 8
MESH = pl.DeviceIdType.MESH
BF = jnp.bfloat16
F32 = jnp.float32
NEG = -1e30
NT = (((1,), (1,)), ((), ()))
TN = (((0,), (0,)), ((), ()))


def iota(shape, dim):
    return lax.broadcasted_iota(jnp.int32, shape, dim)


def kernel(
    n_rep,
    n_tp,
    nx,
    zlo_n,
    hid_hbm,
    proj_hbm,
    idx_ref,
    cnt_ref,
    chg_hbm,
    q_hbm,
    cache_hbm,
    len_ref,
    new_ref,
    att_ref,
    hid,
    proj,
    chg,
    qs,
    cache,
    gath,
    aim,
    perm,
    hp,
    hs,
    hsm,
    d32,
    dd,
    dense,
    acc,
    send1,
    recv1,
    mid,
    send2,
    recv2,
    bias,
    mixed,
    mstat,
    lstat,
    local_sem,
    s1_send,
    s1_recv,
    s2_send,
    s2_recv,
    s3_send,
    s3_recv,
    hs_send,
    hs_recv,
    p1_send,
    p1_recv,
    p2_send,
    p2_recv,
):
    rep = lax.axis_index("rep")
    tp = lax.axis_index("tp")
    core = rep % 2
    z = rep // 2
    nz = n_rep // 2
    zhi_n = nz // zlo_n
    zlo = z % zlo_n
    zhi = z // zlo_n
    ny = n_tp // nx
    y = tp // nx
    x = tp % nx
    ks = BLK // n_tp
    depth = hid.shape[1]
    rows = hid.shape[0]
    nrb = depth // BLK
    kvw = proj.shape[1]
    own_rows = rows // n_tp
    slots = n_rep * SLOTS
    share = nrb * ks
    cw = kvw // 2
    ncb = kvw // BLK
    tile_rows = SLOTS * ks

    loads = []
    for n, (src, dst) in enumerate(
        ((chg_hbm, chg), (hid_hbm, hid), (proj_hbm, proj), (q_hbm, qs), (cache_hbm, cache))
    ):
        copy = pltpu.make_async_copy(src, dst, local_sem.at[n])
        copy.start()
        loads.append(copy)

    sign = 1 - 2 * core

    def at_z(zz, cc):
        return {"rep": ((zz + 2 * nz) % nz) * 2 + cc, "tp": tp}

    def at_plane(o, direction):
        oy, ox = o // nx, o % nx
        return ((y + direction * oy + ny) % ny) * nx + (x + direction * ox + nx) % nx

    strides = list(range(1, zhi_n))
    steps = [d for d in range(-(zlo_n // 2 - 1), zlo_n // 2 + 1) if d != 0]

    barrier = pltpu.get_barrier_semaphore()
    for j in strides:
        pl.semaphore_signal(barrier, inc=1, device_id=at_z(z + zlo_n * j, core), device_id_type=MESH)
    for d in steps:
        pl.semaphore_signal(barrier, inc=1, device_id=at_z(z - sign * d, core), device_id_type=MESH)
    pl.semaphore_signal(barrier, inc=1, device_id=at_z(z, 1 - core), device_id_type=MESH)
    for o in range(1, n_tp):
        pl.semaphore_signal(
            barrier, inc=1, device_id={"rep": rep, "tp": at_plane(o, -1)}, device_id_type=MESH
        )

    place = (core * zlo_n + zlo) * zhi_n + zhi
    lane = iota((1, 128), 1)
    row_value = jnp.zeros((1, 128), F32)
    for s in range(SLOTS):
        b = idx_ref[0, s]
        target = (b & (ncb - 1)) * (n_tp * nrb) + (b >> 4) + 1
        target = jnp.where(s < cnt_ref[0], target, 0)
        row_value = jnp.where(lane == place * SLOTS + s, target.astype(F32), row_value)
    aim[zhi] = row_value

    pj = iota((tile_rows, 1), 0)
    pk = iota((1, SLOTS * BLK), 1)
    pick = jnp.where(pk == (pj // ks) * BLK + tp * ks + pj % ks, 1.0, 0.0).astype(BF)
    loads[0].wait()
    own_share = jnp.dot(pick, chg[...].reshape(SLOTS * BLK, BLK), preferred_element_type=F32)
    gath[core, zlo, zhi] = own_share.astype(BF)

    scale = 1.0 / math.sqrt(HD)

    def head_queries(k):
        heads = qs[:, pl.ds(pl.multiple_of(k * GROUP * HD, GROUP * HD), GROUP * HD)]
        return jnp.concatenate([heads[:, g * HD : (g + 1) * HD] for g in range(GROUP)], axis=0)

    def hs_wait():
        return pltpu.make_async_remote_copy(
            src_ref=hs.at[pl.ds(1, n_tp - 1)],
            dst_ref=hs.at[pl.ds(1, n_tp - 1)],
            send_sem=hs_send,
            recv_sem=hs_recv,
            device_id={"rep": rep, "tp": at_plane(1, 1)},
            device_id_type=MESH,
        )

    def project():
        loads[2].wait()
        tile = 512

        @pl.loop(0, kvw // tile)
        def _(n):
            cols = pl.ds(pl.multiple_of(n * tile, tile), tile)
            acc[:, cols] = jnp.dot(hid[...], proj[:, cols], preferred_element_type=F32)

    def attend_cached():
        loads[3].wait()
        loads[4].wait()
        span = cache.shape[1]
        positions = own_rows * span
        pos_lane = iota((1, positions), 1)
        valid_len = jnp.zeros((1, positions), jnp.int32)
        for i in range(own_rows):
            valid_len = jnp.where(pos_lane // span == i, len_ref[i], valid_len)
        seen = jnp.where(pos_lane % span < valid_len, 0.0, NEG)
        same = (
            iota((GROUP * own_rows, positions), 0) % own_rows
            == iota((GROUP * own_rows, positions), 1) // span
        )
        bias[...] = jnp.where(same, seen, NEG)

        @pl.loop(0, KVH)
        def _(k):
            keys = cache[:, :, pl.ds(pl.multiple_of(k * HD, HD), HD)].reshape(positions, HD)
            values = cache[:, :, pl.ds(pl.multiple_of((KVH + k) * HD, HD), HD)].reshape(positions, HD)
            score = lax.dot_general(head_queries(k), keys, NT, preferred_element_type=F32)
            score = score * scale + bias[...]
            top = jnp.max(score, axis=1, keepdims=True)
            e = jnp.exp(score - top)
            hi = e.astype(BF)
            lo = (e - hi.astype(F32)).astype(BF)
            mixed[k] = jnp.dot(hi, values, preferred_element_type=F32) + jnp.dot(
                lo, values, preferred_element_type=F32
            )
            mstat[k] = jnp.broadcast_to(top, (GROUP * own_rows, HD))
            lstat[k] = jnp.broadcast_to(jnp.sum(e, axis=1, keepdims=True), (GROUP * own_rows, HD))

    early = z < nz // 2

    loads[1].wait()

    @pl.when(early)
    def _():
        project()
        attend_cached()

    pl.semaphore_wait(barrier, len(strides) + len(steps) + 1 + n_tp - 1)

    def far_copies(j, send):
        zz = zhi if send else (zhi - j + zhi_n) % zhi_n
        return [
            pltpu.make_async_remote_copy(
                src_ref=ref,
                dst_ref=ref,
                send_sem=s1_send.at[m, j - 1],
                recv_sem=s1_recv.at[m, j - 1],
                device_id=at_z(z + zlo_n * j, core),
                device_id_type=MESH,
            )
            for m, ref in enumerate((gath.at[core, zlo, zz], aim.at[zz]))
        ]

    def near_copy(i, d, send):
        zz = zlo if send else (zlo - sign * d + zlo_n) % zlo_n
        return pltpu.make_async_remote_copy(
            src_ref=gath.at[core, zz],
            dst_ref=gath.at[core, zz],
            send_sem=s2_send.at[i],
            recv_sem=s2_recv.at[i],
            device_id=at_z(z + sign * d, core),
            device_id_type=MESH,
        )

    def core_copy(send):
        cc = core if send else 1 - core
        return pltpu.make_async_remote_copy(
            src_ref=gath.at[cc],
            dst_ref=gath.at[cc],
            send_sem=s3_send,
            recv_sem=s3_recv,
            device_id=at_z(z, 1 - core),
            device_id_type=MESH,
        )

    for j in strides:
        for copy in far_copies(j, True):
            copy.start()

    pj = iota((depth, 1), 0)
    pk = iota((1, depth), 1)
    p1 = ((pj & (share - 1)) // ks) * BLK + (pj // share) * ks + (pj & (ks - 1))
    perm[...] = jnp.where(p1 == pk, 1.0, 0.0).astype(BF)
    hp[...] = (
        lax.dot_general(perm[...], hid[...], NT, preferred_element_type=F32)
        .astype(BF)
        .reshape(hp.shape)
    )
    hs[0] = hp[tp]
    for o in range(1, n_tp):
        dest = at_plane(o, 1)
        pltpu.make_async_remote_copy(
            src_ref=hp.at[dest],
            dst_ref=hs.at[o],
            send_sem=hs_send,
            recv_sem=hs_recv,
            device_id={"rep": rep, "tp": dest},
            device_id_type=MESH,
        ).start()

    for j in strides:
        for copy in far_copies(j, False):
            copy.wait_recv()
    aims = jnp.sum(aim[...].reshape(zhi_n, 128), axis=0, keepdims=True)
    upper = jnp.floor(aims * (1.0 / 32.0))
    line = iota((tile_rows, 128), 0)
    gath[core, zlo, zhi_n] = jnp.where(
        line == 0, upper, jnp.where(line == 1, aims - 32.0 * upper, 0.0)
    ).astype(BF)
    for i, d in enumerate(steps):
        near_copy(i, d, True).start()

    @pl.when(jnp.logical_not(early))
    def _():
        project()

    pj = iota((depth, 1), 0)
    pk = iota((1, depth), 1)
    po = pj // share
    pc = ((y - po // nx + ny) & (ny - 1)) * nx + ((x - (po & (nx - 1)) + nx) & (nx - 1))
    p2 = (pj & (ks - 1)) * (n_tp * nrb) + pc * nrb + (pj & (share - 1)) // ks
    perm[...] = jnp.where(p2 == pk, 1.0, 0.0).astype(BF)

    for i, d in enumerate(steps):
        near_copy(i, d, False).wait_recv()
    core_copy(True).start()
    hs_wait().wait_recv()
    hsm[...] = lax.dot_general(
        hs[...].reshape(depth, rows), perm[...], TN, preferred_element_type=F32
    ).astype(BF)

    core_copy(False).wait_recv()

    code = jnp.sum(gath[:, :, zhi_n].reshape(2 * zlo_n, tile_rows, 128).astype(F32), axis=0)
    target_row = (code[0:1] * 32.0 + code[1:2])[:, :slots]
    d32[...] = gath[:, :, :zhi_n].reshape(slots * ks, BLK).astype(F32)
    for k in range(ks):
        dd[:, k * BLK : (k + 1) * BLK] = d32[pl.ds(k, slots, stride=ks), :].astype(BF)

    per = cw // BLK
    grp = n_tp * nrb

    def one_axis(h, phase, o):
        along_x = (h + phase) % 2 == 0
        size = nx if along_x else ny
        at = (((x if along_x else y) + o) % size).astype(jnp.int32)
        return size, at, (y * nx + at if along_x else at * nx + x)

    def first_copies(h):
        size = one_axis(h, 0, 0)[0]
        made = []
        for o in range(1, size):
            _, at, dest = one_axis(h, 0, o)
            made.append(
                pltpu.make_async_remote_copy(
                    src_ref=send1.at[h, at],
                    dst_ref=recv1.at[h, o - 1],
                    send_sem=p1_send.at[h, o - 1],
                    recv_sem=p1_recv.at[h, o - 1],
                    device_id={"rep": rep, "tp": dest},
                    device_id_type=MESH,
                )
            )
        return made

    def second_copies(h):
        size = one_axis(h, 1, 0)[0]
        made = []
        for o in range(1, size):
            _, at, dest = one_axis(h, 1, o)
            made.append(
                pltpu.make_async_remote_copy(
                    src_ref=send2.at[h, at],
                    dst_ref=recv2.at[h, o - 1],
                    send_sem=p2_send.at[h, o - 1],
                    recv_sem=p2_recv.at[h, o - 1],
                    device_id={"rep": rep, "tp": dest},
                    device_id_type=MESH,
                )
            )
        return made

    for h in range(2):
        ids = (iota((per * grp, slots), 0) + (h * per * grp + 1)).astype(F32)
        onehot = jnp.where(ids == target_row, 1.0, 0.0).astype(BF)
        for k in range(0, ks, 2):
            placed = jnp.dot(
                onehot, dd[:, k * BLK : (k + 2) * BLK], preferred_element_type=F32
            ).astype(BF)
            for c in range(per):
                for i in range(2):
                    dense[(k + i) * grp : (k + i + 1) * grp, c * BLK : (c + 1) * BLK] = placed[
                        c * grp : (c + 1) * grp, i * BLK : (i + 1) * BLK
                    ]
        wide = 256
        for n in range(cw // wide):
            cols = slice(h * cw + n * wide, h * cw + (n + 1) * wide)
            there = slice(n * wide, (n + 1) * wide)
            total = acc[:, cols] + jnp.dot(hsm[...], dense[:, there], preferred_element_type=F32)
            acc[:, cols] = total
            part = total.astype(BF).reshape(ny, nx, own_rows, wide)
            for yy in range(ny):
                if h == 0:
                    for xx in range(nx):
                        send1[h, xx, yy, :, there] = part[yy, xx]
                else:
                    send1[h, yy, :, :, there] = part[yy]
        for copy in first_copies(h):
            copy.start()

    @pl.when(jnp.logical_not(early))
    def _():
        attend_cached()

    for h in range(2):
        copies = first_copies(h)
        for copy in copies:
            copy.wait_recv()
        cols = slice(h * cw, (h + 1) * cw)
        for a in range(ny if h == 0 else nx):
            row = (a * nx + x if h == 0 else y * nx + a) * own_rows
            total = acc[pl.ds(pl.multiple_of(row, own_rows), own_rows), cols]
            for n in range(len(copies)):
                total = total + recv1[h, n, a].astype(F32)
            mid[h, a] = total
            send2[h, a] = total.astype(BF)
        for copy in second_copies(h):
            copy.start()
    def finish(h):
        copies = second_copies(h)
        for copy in copies:
            copy.wait_recv()
        total = mid[h, y if h == 0 else x]
        for n in range(len(copies)):
            total = total + recv2[h, n].astype(F32)
        new_ref[:, h * cw : (h + 1) * cw] = total.astype(BF)

    finish(0)
    for k in range(KVH):
        own_key = new_ref[:, k * HD : (k + 1) * HD].astype(F32)
        own = (
            jnp.sum(
                head_queries(k).astype(F32) * jnp.concatenate([own_key] * GROUP, axis=0),
                axis=1,
                keepdims=True,
            )
            * scale
        )
        top = mstat[k]
        new_top = jnp.maximum(top, own)
        a = jnp.exp(top - new_top)
        b = jnp.exp(own - new_top)
        inv = 1.0 / (lstat[k] * a + b)
        mixed[k] = mixed[k] * (a * inv)
        lstat[k] = b * inv
    finish(1)
    for k in range(KVH):
        own_value = new_ref[:, (KVH + k) * HD : (KVH + k + 1) * HD].astype(F32)
        out = mixed[k] + lstat[k] * jnp.concatenate([own_value] * GROUP, axis=0)
        out = out.astype(BF)
        for g in range(GROUP):
            at = (k * GROUP + g) * HD
            att_ref[:, at : at + HD] = out[g * own_rows : (g + 1) * own_rows]

    for j in strides:
        for copy in far_copies(j, True):
            copy.wait_send()
    for i, d in enumerate(steps):
        near_copy(i, d, True).wait_send()
    core_copy(True).wait_send()
    hs_wait().wait_send()
    for h in range(2):
        for copy in first_copies(h) + second_copies(h):
            copy.wait_send()


def solution(mesh):
    n_rep, n_tp = mesh.shape["rep"], mesh.shape["tp"]
    nx = 4 if n_tp == 16 else 2
    nz = n_rep // 2
    zlo_n = 8 if nz == 32 else 2
    zhi_n = nz // zlo_n

    def body(hidden, projection, block_index, block_counts, block_change, queries, cached, lengths):
        rows, depth = hidden.shape
        kvw = projection.shape[1]
        own_rows, span = cached.shape[0], cached.shape[1]
        ks = BLK // n_tp
        slots = n_rep * SLOTS
        share = depth // n_tp
        cw = kvw // 2
        heads = GROUP * own_rows
        n2 = zlo_n - 1
        side = nx
        any_spec = pl.BlockSpec(memory_space=pl.ANY)
        smem = pl.BlockSpec(memory_space=pltpu.SMEM)
        vmem = pl.BlockSpec(memory_space=pltpu.VMEM)
        dma = pltpu.SemaphoreType.DMA
        return pl.pallas_call(
            functools.partial(kernel, n_rep, n_tp, nx, zlo_n),
            out_shape=(
                jax.ShapeDtypeStruct((own_rows, kvw), BF),
                jax.ShapeDtypeStruct((own_rows, queries.shape[1]), BF),
            ),
            in_specs=[any_spec, any_spec, smem, smem, any_spec, any_spec, any_spec, smem],
            out_specs=(vmem, vmem),
            scratch_shapes=[
                pltpu.VMEM((rows, depth), BF),
                pltpu.VMEM((depth, kvw), BF),
                pltpu.VMEM(block_change.shape, BF),
                pltpu.VMEM(queries.shape, BF),
                pltpu.VMEM(cached.shape, BF),
                pltpu.VMEM((2, zlo_n, zhi_n + 1, SLOTS * ks, BLK), BF),
                pltpu.VMEM((zhi_n, 1, 128), F32),
                pltpu.VMEM((depth, depth), BF),
                pltpu.VMEM((n_tp, share, rows), BF),
                pltpu.VMEM((n_tp, share, rows), BF),
                pltpu.VMEM((rows, depth), BF),
                pltpu.VMEM((slots * ks, BLK), F32),
                pltpu.VMEM((slots, ks * BLK), BF),
                pltpu.VMEM((depth, cw), BF),
                pltpu.VMEM((rows, kvw), F32),
                pltpu.VMEM((2, side, side, own_rows, cw), BF),
                pltpu.VMEM((2, side - 1, side, own_rows, cw), BF),
                pltpu.VMEM((2, side, own_rows, cw), F32),
                pltpu.VMEM((2, side, own_rows, cw), BF),
                pltpu.VMEM((2, side - 1, own_rows, cw), BF),
                pltpu.VMEM((heads, own_rows * span), F32),
                pltpu.VMEM((KVH, heads, HD), F32),
                pltpu.VMEM((KVH, heads, HD), F32),
                pltpu.VMEM((KVH, heads, HD), F32),
                dma((5,)),
                dma((2, zhi_n - 1)),
                dma((2, zhi_n - 1)),
                dma((n2,)),
                dma((n2,)),
                dma,
                dma,
                dma,
                dma,
                dma((2, side - 1)),
                dma((2, side - 1)),
                dma((2, side - 1)),
                dma((2, side - 1)),
            ],
            compiler_params=pltpu.CompilerParams(
                collective_id=0, has_side_effects=True, vmem_limit_bytes=60 * 1024 * 1024
            ),
        )(hidden, projection, block_index, block_counts, block_change, queries, cached, lengths)

    return jax.shard_map(
        body,
        mesh=mesh,
        in_specs=(
            P("rep", "tp"),
            P("tp", None),
            P("rep", None),
            P("rep"),
            P("rep", None, None, None),
            P(("rep", "tp"), None),
            P(("rep", "tp"), None, None),
            P(("rep", "tp")),
        ),
        out_specs=(P(("rep", "tp"), None), P(("rep", "tp"), None)),
        check_vma=False,
    )
```

time: 75.9 us -> 68.3 us (0.90)
  local copies, waits for them, and re-layouts: 8.56 us -> 3.14 us
  Pallas kernels: 65.7 us -> 63.6 us
    unnamed x16 -> x2, local copies, waits for them, and re-layouts: 8.56 us -> 3.14 us
    pallas_call x1, Pallas kernels: 65.7 us -> 63.6 us  [body(): pl.pallas_call(functools.partial(kernel, n_rep, n_tp, nx, zlo_n), out_sha...]
where the time goes in v2:
time: 68.3 us; the launch traced here: 68 us
  Pallas kernels  63.6 us (93%)
  local copies, waits for them, and re-layouts  3.14 us (5%)
  between operations  1.29 us (2%)
    pallas_call x1, Pallas kernels, body(): pl.pallas_call(functools.partial(kernel, n_rep, n_tp, nx, zlo_n), out_sha...  63.6 us
    unnamed x2, local copies, waits for them, and re-layouts  3.14 us

profile of v2, /device:TPU:1, one launch (start us, length us, event | category | flops | bytes accessed | tf_op | source)
XLA Modules:
  0.0 68.0 jit_solution(16510725487152843921)
XLA Ops:
  1.3 63.6 %shard_map.95 = (bf16[16,2048]{1,0:T(8,128)(2,1)}, bf16[16,8192]{1,0:T(8,128)(2,1)}) custom-call(bf16[256,512]{1,0:T(8,128)(2,1)} %hid_hbm.1, bf16[512,2048]{1,0:T(8,128)(2,1)} %proj_hbm.1, s32[1,2]{1,0:T(1,128)} %idx_ref.1, s32[1]{0:T(128)S(6)} %copy.12.cnt_ref, bf16[1,2,128,128]{3,2,1,0:T(8,128)(2,1)} %chg_hbm.1, bf16[16,8192]{1,0:T(8,128)(2,1)} %q_hbm.1, ...), custom_call_target="tpu_custom_call" | custom-call | tf_op jit(solution)/shard_map/pallas_call | solution.py:480
  64.9 1.5 %copy.13 = bf16[16,2048]{1,0:T(8,128)(2,1)} copy(bf16[16,2048]{1,0:T(8,128)(2,1)} %get-tuple-element.4) | data formatting | bytes 131072
  66.4 1.7 %copy.14 = bf16[16,8192]{1,0:T(8,128)(2,1)} copy(bf16[16,8192]{1,0:T(8,128)(2,1)} %get-tuple-element.5) | data formatting | bytes 524288

commit v3 on v2

--- a/solution.py
+++ b/solution.py
@@ -98,7 +98,8 @@
     own_rows = rows // n_tp
     slots = n_rep * SLOTS
     share = nrb * ks
-    cw = kvw // 2
+    parts = 2
+    cw = kvw // (2 * parts)
     ncb = kvw // BLK
     tile_rows = SLOTS * ks
 
@@ -119,8 +120,9 @@
         oy, ox = o // nx, o % nx
         return ((y + direction * oy + ny) % ny) * nx + (x + direction * ox + nx) % nx
 
-    strides = list(range(1, zhi_n))
+    strides = sorted(range(1, zhi_n), key=lambda j: -min(j, zhi_n - j))
     steps = [d for d in range(-(zlo_n // 2 - 1), zlo_n // 2 + 1) if d != 0]
+    steps.sort(key=lambda d: -abs(d))
 
     barrier = pltpu.get_barrier_semaphore()
     for j in strides:
@@ -207,7 +209,7 @@
             mstat[k] = jnp.broadcast_to(top, (GROUP * own_rows, HD))
             lstat[k] = jnp.broadcast_to(jnp.sum(e, axis=1, keepdims=True), (GROUP * own_rows, HD))
 
-    early = z < nz // 2
+    early = z < (3 * nz) // 8
 
     loads[1].wait()
 
@@ -243,13 +245,13 @@
             device_id_type=MESH,
         )
 
-    def core_copy(send):
+    def core_copy(zz, send):
         cc = core if send else 1 - core
         return pltpu.make_async_remote_copy(
-            src_ref=gath.at[cc],
-            dst_ref=gath.at[cc],
-            send_sem=s3_send,
-            recv_sem=s3_recv,
+            src_ref=gath.at[cc, zz],
+            dst_ref=gath.at[cc, zz],
+            send_sem=s3_send.at[zz],
+            recv_sem=s3_recv.at[zz],
             device_id=at_z(z, 1 - core),
             device_id_type=MESH,
         )
@@ -290,6 +292,7 @@
     ).astype(BF)
     for i, d in enumerate(steps):
         near_copy(i, d, True).start()
+    core_copy(zlo, True).start()
 
     @pl.when(jnp.logical_not(early))
     def _():
@@ -302,15 +305,16 @@
     p2 = (pj & (ks - 1)) * (n_tp * nrb) + pc * nrb + (pj & (share - 1)) // ks
     perm[...] = jnp.where(p2 == pk, 1.0, 0.0).astype(BF)
 
-    for i, d in enumerate(steps):
+    for i, d in reversed(list(enumerate(steps))):
         near_copy(i, d, False).wait_recv()
-    core_copy(True).start()
+        core_copy((zlo - sign * d + zlo_n) % zlo_n, True).start()
     hs_wait().wait_recv()
     hsm[...] = lax.dot_general(
         hs[...].reshape(depth, rows), perm[...], TN, preferred_element_type=F32
     ).astype(BF)
 
-    core_copy(False).wait_recv()
+    for zz in range(zlo_n):
+        core_copy(zz, False).wait_recv()
 
     code = jnp.sum(gath[:, :, zhi_n].reshape(2 * zlo_n, tile_rows, 128).astype(F32), axis=0)
     target_row = (code[0:1] * 32.0 + code[1:2])[:, :slots]
@@ -323,59 +327,45 @@
 
     def one_axis(h, phase, o):
         along_x = (h + phase) % 2 == 0
-        size = nx if along_x else ny
-        at = (((x if along_x else y) + o) % size).astype(jnp.int32)
-        return size, at, (y * nx + at if along_x else at * nx + x)
-
-    def first_copies(h):
-        size = one_axis(h, 0, 0)[0]
+        at = ((x if along_x else y) + o) % (nx if along_x else ny)
+        return at, (y * nx + at if along_x else at * nx + x)
+
+    def copies(h, c, phase):
+        src, dst, sent, got = (
+            (send1, recv1, p1_send, p1_recv) if phase == 0 else (send2, recv2, p2_send, p2_recv)
+        )
         made = []
-        for o in range(1, size):
-            _, at, dest = one_axis(h, 0, o)
+        for o in sorted(range(1, nx), key=lambda o: -min(o, nx - o)):
+            at, dest = one_axis(h, phase, o)
             made.append(
                 pltpu.make_async_remote_copy(
-                    src_ref=send1.at[h, at],
-                    dst_ref=recv1.at[h, o - 1],
-                    send_sem=p1_send.at[h, o - 1],
-                    recv_sem=p1_recv.at[h, o - 1],
+                    src_ref=src.at[h * parts + c, at],
+                    dst_ref=dst.at[h * parts + c, o - 1],
+                    send_sem=sent.at[h * parts + c, o - 1],
+                    recv_sem=got.at[h * parts + c, o - 1],
                     device_id={"rep": rep, "tp": dest},
                     device_id_type=MESH,
                 )
             )
         return made
 
-    def second_copies(h):
-        size = one_axis(h, 1, 0)[0]
-        made = []
-        for o in range(1, size):
-            _, at, dest = one_axis(h, 1, o)
-            made.append(
-                pltpu.make_async_remote_copy(
-                    src_ref=send2.at[h, at],
-                    dst_ref=recv2.at[h, o - 1],
-                    send_sem=p2_send.at[h, o - 1],
-                    recv_sem=p2_recv.at[h, o - 1],
-                    device_id={"rep": rep, "tp": dest},
-                    device_id_type=MESH,
-                )
-            )
-        return made
-
-    for h in range(2):
-        ids = (iota((per * grp, slots), 0) + (h * per * grp + 1)).astype(F32)
+    wide = 256
+    chunks = [(h, c) for c in range(parts) for h in range(2)]
+    for h, c in chunks:
+        hc = h * parts + c
+        ids = (iota((per * grp, slots), 0) + (hc * per * grp + 1)).astype(F32)
         onehot = jnp.where(ids == target_row, 1.0, 0.0).astype(BF)
         for k in range(0, ks, 2):
             placed = jnp.dot(
                 onehot, dd[:, k * BLK : (k + 2) * BLK], preferred_element_type=F32
             ).astype(BF)
-            for c in range(per):
+            for b in range(per):
                 for i in range(2):
-                    dense[(k + i) * grp : (k + i + 1) * grp, c * BLK : (c + 1) * BLK] = placed[
-                        c * grp : (c + 1) * grp, i * BLK : (i + 1) * BLK
+                    dense[(k + i) * grp : (k + i + 1) * grp, b * BLK : (b + 1) * BLK] = placed[
+                        b * grp : (b + 1) * grp, i * BLK : (i + 1) * BLK
                     ]
-        wide = 256
         for n in range(cw // wide):
-            cols = slice(h * cw + n * wide, h * cw + (n + 1) * wide)
+            cols = slice(hc * cw + n * wide, hc * cw + (n + 1) * wide)
             there = slice(n * wide, (n + 1) * wide)
             total = acc[:, cols] + jnp.dot(hsm[...], dense[:, there], preferred_element_type=F32)
             acc[:, cols] = total
@@ -383,38 +373,40 @@
             for yy in range(ny):
                 if h == 0:
                     for xx in range(nx):
-                        send1[h, xx, yy, :, there] = part[yy, xx]
+                        send1[hc, xx, yy, :, there] = part[yy, xx]
                 else:
-                    send1[h, yy, :, :, there] = part[yy]
-        for copy in first_copies(h):
+                    send1[hc, yy, :, :, there] = part[yy]
+        for copy in copies(h, c, 0):
             copy.start()
 
     @pl.when(jnp.logical_not(early))
     def _():
         attend_cached()
 
-    for h in range(2):
-        copies = first_copies(h)
-        for copy in copies:
+    for h, c in chunks:
+        hc = h * parts + c
+        for copy in copies(h, c, 0):
             copy.wait_recv()
-        cols = slice(h * cw, (h + 1) * cw)
-        for a in range(ny if h == 0 else nx):
+        cols = slice(hc * cw, (hc + 1) * cw)
+        for a in range(nx):
             row = (a * nx + x if h == 0 else y * nx + a) * own_rows
             total = acc[pl.ds(pl.multiple_of(row, own_rows), own_rows), cols]
-            for n in range(len(copies)):
-                total = total + recv1[h, n, a].astype(F32)
-            mid[h, a] = total
-            send2[h, a] = total.astype(BF)
-        for copy in second_copies(h):
+            for n in range(nx - 1):
+                total = total + recv1[hc, n, a].astype(F32)
+            mid[hc, a] = total
+            send2[hc, a] = total.astype(BF)
+        for copy in copies(h, c, 1):
             copy.start()
+
     def finish(h):
-        copies = second_copies(h)
-        for copy in copies:
-            copy.wait_recv()
-        total = mid[h, y if h == 0 else x]
-        for n in range(len(copies)):
-            total = total + recv2[h, n].astype(F32)
-        new_ref[:, h * cw : (h + 1) * cw] = total.astype(BF)
+        for c in range(parts):
+            hc = h * parts + c
+            for copy in copies(h, c, 1):
+                copy.wait_recv()
+            total = mid[hc, y if h == 0 else x]
+            for n in range(nx - 1):
+                total = total + recv2[hc, n].astype(F32)
+            new_ref[:, hc * cw : (hc + 1) * cw] = total.astype(BF)
 
     finish(0)
     for k in range(KVH):
@@ -448,10 +440,11 @@
             copy.wait_send()
     for i, d in enumerate(steps):
         near_copy(i, d, True).wait_send()
-    core_copy(True).wait_send()
+    for zz in range(zlo_n):
+        core_copy(zz, True).wait_send()
     hs_wait().wait_send()
-    for h in range(2):
-        for copy in first_copies(h) + second_copies(h):
+    for h, c in chunks:
+        for copy in copies(h, c, 0) + copies(h, c, 1):
             copy.wait_send()
 
 
@@ -469,7 +462,8 @@
         ks = BLK // n_tp
         slots = n_rep * SLOTS
         share = depth // n_tp
-        cw = kvw // 2
+        parts = 4
+        cw = kvw // parts
         heads = GROUP * own_rows
         n2 = zlo_n - 1
         side = nx
@@ -501,11 +495,11 @@
                 pltpu.VMEM((slots, ks * BLK), BF),
                 pltpu.VMEM((depth, cw), BF),
                 pltpu.VMEM((rows, kvw), F32),
-                pltpu.VMEM((2, side, side, own_rows, cw), BF),
-                pltpu.VMEM((2, side - 1, side, own_rows, cw), BF),
-                pltpu.VMEM((2, side, own_rows, cw), F32),
-                pltpu.VMEM((2, side, own_rows, cw), BF),
-                pltpu.VMEM((2, side - 1, own_rows, cw), BF),
+                pltpu.VMEM((parts, side, side, own_rows, cw), BF),
+                pltpu.VMEM((parts, side - 1, side, own_rows, cw), BF),
+                pltpu.VMEM((parts, side, own_rows, cw), F32),
+                pltpu.VMEM((parts, side, own_rows, cw), BF),
+                pltpu.VMEM((parts, side - 1, own_rows, cw), BF),
                 pltpu.VMEM((heads, own_rows * span), F32),
                 pltpu.VMEM((KVH, heads, HD), F32),
                 pltpu.VMEM((KVH, heads, HD), F32),
@@ -515,14 +509,14 @@
                 dma((2, zhi_n - 1)),
                 dma((n2,)),
                 dma((n2,)),
+                dma((zlo_n,)),
+                dma((zlo_n,)),
                 dma,
                 dma,
-                dma,
-                dma,
-                dma((2, side - 1)),
-                dma((2, side - 1)),
-                dma((2, side - 1)),
-                dma((2, side - 1)),
+                dma((parts, side - 1)),
+                dma((parts, side - 1)),
+                dma((parts, side - 1)),
+                dma((parts, side - 1)),
             ],
             compiler_params=pltpu.CompilerParams(
                 collective_id=0, has_side_effects=True, vmem_limit_bytes=60 * 1024 * 1024

time: 68.3 us -> 67.8 us (level)
  no operation moved by 1% of the time
where the time goes in v3:
time: 67.8 us; the launch traced here: 67.6 us
  Pallas kernels  63.1 us (93%)
  local copies, waits for them, and re-layouts  3.14 us (5%)
  between operations  1.29 us (2%)
    pallas_call x1, Pallas kernels, body(): pl.pallas_call(functools.partial(kernel, n_rep, n_tp, nx, zlo_n), out_sha...  63.1 us
    unnamed x2, local copies, waits for them, and re-layouts  3.14 us

profile of v3, /device:TPU:1, one launch (start us, length us, event | category | flops | bytes accessed | tf_op | source)
XLA Modules:
  0.0 67.6 jit_solution(13838529483678769885)
XLA Ops:
  1.3 63.1 %shard_map.95 = (bf16[16,2048]{1,0:T(8,128)(2,1)}, bf16[16,8192]{1,0:T(8,128)(2,1)}) custom-call(bf16[256,512]{1,0:T(8,128)(2,1)} %hid_hbm.1, bf16[512,2048]{1,0:T(8,128)(2,1)} %proj_hbm.1, s32[1,2]{1,0:T(1,128)} %idx_ref.1, s32[1]{0:T(128)S(6)} %copy.12.cnt_ref, bf16[1,2,128,128]{3,2,1,0:T(8,128)(2,1)} %chg_hbm.1, bf16[16,8192]{1,0:T(8,128)(2,1)} %q_hbm.1, ...), custom_call_target="tpu_custom_call" | custom-call | tf_op jit(solution)/shard_map/pallas_call | solution.py:474
  64.4 1.5 %copy.13 = bf16[16,2048]{1,0:T(8,128)(2,1)} copy(bf16[16,2048]{1,0:T(8,128)(2,1)} %get-tuple-element.4) | data formatting | bytes 131072
  65.9 1.7 %copy.14 = bf16[16,8192]{1,0:T(8,128)(2,1)} copy(bf16[16,8192]{1,0:T(8,128)(2,1)} %get-tuple-element.5) | data formatting | bytes 524288

commit v4 on v3

--- a/solution.py
+++ b/solution.py
@@ -452,7 +452,7 @@
     n_rep, n_tp = mesh.shape["rep"], mesh.shape["tp"]
     nx = 4 if n_tp == 16 else 2
     nz = n_rep // 2
-    zlo_n = 8 if nz == 32 else 2
+    zlo_n = 4 if nz == 32 else 2
     zhi_n = nz // zlo_n
 
     def body(hidden, projection, block_index, block_counts, block_change, queries, cached, lengths):

time: 67.8 us -> 67.1 us (0.990)
  Pallas kernels: 63.1 us -> 62.4 us
    pallas_call x1, Pallas kernels: 63.1 us -> 62.4 us  [body(): pl.pallas_call(functools.partial(kernel, n_rep, n_tp, nx, zlo_n), out_sha...]
where the time goes in v4:
time: 67.1 us; the launch traced here: 66.9 us
  Pallas kernels  62.4 us (93%)
  local copies, waits for them, and re-layouts  3.14 us (5%)
  between operations  1.29 us (2%)
    pallas_call x1, Pallas kernels, body(): pl.pallas_call(functools.partial(kernel, n_rep, n_tp, nx, zlo_n), out_sha...  62.4 us
    unnamed x2, local copies, waits for them, and re-layouts  3.14 us

profile of v4, /device:TPU:1, one launch (start us, length us, event | category | flops | bytes accessed | tf_op | source)
XLA Modules:
  0.0 66.9 jit_solution(9272327349108133107)
XLA Ops:
  1.3 62.4 %shard_map.95 = (bf16[16,2048]{1,0:T(8,128)(2,1)}, bf16[16,8192]{1,0:T(8,128)(2,1)}) custom-call(bf16[256,512]{1,0:T(8,128)(2,1)} %hid_hbm.1, bf16[512,2048]{1,0:T(8,128)(2,1)} %proj_hbm.1, s32[1,2]{1,0:T(1,128)} %idx_ref.1, s32[1]{0:T(128)S(6)} %copy.12.cnt_ref, bf16[1,2,128,128]{3,2,1,0:T(8,128)(2,1)} %chg_hbm.1, bf16[16,8192]{1,0:T(8,128)(2,1)} %q_hbm.1, ...), custom_call_target="tpu_custom_call" | custom-call | tf_op jit(solution)/shard_map/pallas_call | solution.py:474
  63.7 1.5 %copy.13 = bf16[16,2048]{1,0:T(8,128)(2,1)} copy(bf16[16,2048]{1,0:T(8,128)(2,1)} %get-tuple-element.4) | data formatting | bytes 131072
  65.2 1.7 %copy.14 = bf16[16,8192]{1,0:T(8,128)(2,1)} copy(bf16[16,8192]{1,0:T(8,128)(2,1)} %get-tuple-element.5) | data formatting | bytes 524288
